TPU v7x, 128 devices: a whole 4x4x4 slice. The times are simulated.
128 devices in a mesh: grp: 4 (over y), seq: 32 (over z, x, core).
Axes of the slice: x: 4, y: 4, z: 4, core: 2. Of those that a mesh axis runs over, the one named last changes fastest.
Arguments:
- byte_ids: int32 [4, 4096], P('grp', 'seq'), may hold values from 0 to 255
- patch_lengths: int32 [4, 256], P('grp'), may hold values from 1 to 32, 4096 in all within a row
- patch_owner: int32 [4, 256], P('grp'), may hold values from 0 to 31, as said below
- emb_table: bfloat16 [256, 1024], replicated, may hold values from -6 to 6
- enc_gain: float32 [1024], replicated, may hold values from 0.1 to 1.9
- w_in: bfloat16 [1024, 4096], P(None, 'seq'), may hold values from -0.1875 to 0.1875
- lat_gain: float32 [4096], replicated, may hold values from 0.1 to 1.9
- w_gate: bfloat16 [14336, 4096], P(('grp', 'seq')), may hold values from -0.09375 to 0.09375
- w_up: bfloat16 [14336, 4096], P(('grp', 'seq')), may hold values from -0.09375 to 0.09375
- w_down: bfloat16 [14336, 4096], P(('grp', 'seq')), may hold values from -0.046875 to 0.046875
- grad_out: bfloat16 [4, 32, 8, 4096], P('grp', 'seq'), may hold values from -6 to 6
Outputs:
- patch_out: bfloat16 [4, 32, 8, 4096], P('grp', 'seq')
- d_emb: float32 [256, 1024], replicated
- d_enc_gain: float32 [1024], replicated
- d_w_in: float32 [1024, 4096], P(None, 'seq')
- d_lat_gain: float32 [4096], replicated
- d_w_gate: float32 [14336, 4096], P(('grp', 'seq'))
- d_w_up: float32 [14336, 4096], P(('grp', 'seq'))
- d_w_down: float32 [14336, 4096], P(('grp', 'seq'))
Inputs may be any that keep to these rules, and one draw needn't show every extreme that they name: `patch_owner`: in each sequence every owner number appears exactly 8 times. `patch_lengths`: each sequence's lengths sum to 4096; the longest is exactly 32.
All inputs are finite; a program needn't handle non-finite values.
Results may differ from a plain program's by a relative error of at most 0.02.
Values may be sent and summed in bfloat16 or wider, within the bound.
No kernel may reach another device: no remote copies, remote signals or barrier semaphores. Data moves between devices by JAX's collectives and lax.ppermute only.
A program may use at most 192 MiB of HBM per device.

v0:
```python
import jax
import jax.numpy as jnp
from jax import lax
from jax.sharding import PartitionSpec as P


def rms_scale(values):
    return lax.rsqrt(jnp.mean(values * values, axis=-1, keepdims=True) + 1e-05)


def silu_parts(gate):
    sigma = jax.nn.sigmoid(gate)
    return (gate * sigma, sigma * (1.0 + gate * (1.0 - sigma)))


def owner_slots(lengths, owners, owner_count, per_owner):
    count = lengths.shape[0]
    onehot_own = (owners[:, None] == jnp.arange(owner_count, dtype=jnp.int32)[None, :]).astype(
        jnp.int32
    )
    rank = jnp.sum((jnp.cumsum(onehot_own, axis=0) - onehot_own) * onehot_own, axis=1)
    target = owners * per_owner + rank
    placed = target[None, :] == jnp.arange(count, dtype=jnp.int32)[:, None]
    starts = jnp.cumsum(lengths) - lengths
    slot_start = jnp.sum(jnp.where(placed, starts[None, :], 0), axis=1)
    slot_len = jnp.sum(jnp.where(placed, lengths[None, :], 0), axis=1)
    return (slot_start, slot_len)


def contract_last(left, right):
    return lax.dot_general(
        left, right, (((1,), (1,)), ((), ())), preferred_element_type=jnp.float32
    )


def contract_first(left, right):
    return lax.dot_general(
        left, right, (((0,), (0,)), ((), ())), preferred_element_type=jnp.float32
    )


def latent_forward(rows, lat_gain, gate_rows, up_rows):
    normed = (rows.astype(jnp.float32) * rms_scale(rows.astype(jnp.float32)) * lat_gain).astype(
        jnp.bfloat16
    )
    gate = contract_last(normed, gate_rows)
    upper = contract_last(normed, up_rows)
    active, slope = silu_parts(gate)
    hidden = (active * upper).astype(jnp.bfloat16)
    return (normed, upper, active, slope, hidden)


def latent_backward(cot_all, normed, upper, active, slope, hidden, down_rows):
    weight_down = contract_first(hidden, cot_all)
    dhid = contract_last(cot_all, down_rows)
    dgate = (dhid * upper * slope).astype(jnp.bfloat16)
    dup = (dhid * active).astype(jnp.bfloat16)
    weight_gate = contract_first(dgate, normed)
    weight_up = contract_first(dup, normed)
    return (weight_gate, weight_up, weight_down, dgate, dup)


def on_device(
    byte_ids,
    patch_lengths,
    patch_owner,
    emb_table,
    enc_gain,
    w_in,
    lat_gain,
    w_gate,
    w_up,
    w_down,
    grad_out,
):
    seq_count = lax.axis_size("seq")
    per_owner = grad_out.shape[2]
    ids = byte_ids[0]
    span = ids.shape[0]
    slot_start, slot_len = owner_slots(patch_lengths[0], patch_owner[0], seq_count, per_owner)
    position = lax.axis_index("seq") * span + jnp.arange(span, dtype=jnp.int32)
    member = (position[None, :] >= slot_start[:, None]) & (
        position[None, :] < (slot_start + slot_len)[:, None]
    )
    onehot_ids = ids[:, None] == jnp.arange(emb_table.shape[0], dtype=jnp.int32)[None, :]
    embedded = jnp.dot(
        onehot_ids.astype(jnp.bfloat16), emb_table, preferred_element_type=jnp.float32
    )
    enc_rms = rms_scale(embedded)
    unit = embedded * enc_rms
    enc = (unit * enc_gain).astype(jnp.bfloat16)
    partial_pool = jnp.dot(member.astype(jnp.bfloat16), enc, preferred_element_type=jnp.float32)
    pooled_sum = lax.psum(partial_pool, "seq")
    lens_f = slot_len.astype(jnp.float32)[:, None]
    pooled = (pooled_sum / lens_f).astype(jnp.bfloat16)
    latent_part = jnp.dot(pooled, w_in, preferred_element_type=jnp.float32).astype(jnp.bfloat16)
    latent = lax.all_gather(latent_part, "seq", axis=1, tiled=True)
    own_lat = lax.dynamic_slice_in_dim(
        latent, lax.axis_index("seq") * per_owner, per_owner, 0
    ).astype(jnp.float32)
    cot_own = grad_out[0, 0]
    rows = lax.all_gather(latent, "grp", axis=0, tiled=True)
    normed, upper, active, slope, hidden = latent_forward(rows, lat_gain, w_gate, w_up)
    mlp_own = lax.psum_scatter(
        jnp.dot(hidden, w_down, preferred_element_type=jnp.float32),
        ("grp", "seq"),
        scatter_dimension=0,
        tiled=True,
    )
    cot_all = lax.all_gather(cot_own, ("grp", "seq"), axis=0, tiled=True)
    d_wg, d_wu, d_wd, dgate, dup = latent_backward(
        cot_all, normed, upper, active, slope, hidden, w_down
    )
    dnormed = lax.psum_scatter(
        jnp.dot(dgate, w_gate, preferred_element_type=jnp.float32)
        + jnp.dot(dup, w_up, preferred_element_type=jnp.float32),
        ("grp", "seq"),
        scatter_dimension=0,
        tiled=True,
    )
    patch_rows = (own_lat + mlp_own).astype(jnp.bfloat16)
    lat_rms = rms_scale(own_lat)
    unit_l = own_lat * lat_rms
    lat_part = jnp.sum(dnormed * unit_l, axis=0)
    scaled = dnormed * lat_gain
    dlatent = (
        cot_own.astype(jnp.float32)
        + lat_rms * (scaled - unit_l * jnp.mean(scaled * unit_l, axis=-1, keepdims=True))
    ).astype(jnp.bfloat16)
    dlatent_cols = lax.all_to_all(dlatent, "seq", split_axis=1, concat_axis=0, tiled=True)
    win_part = contract_first(pooled, dlatent_cols)
    pool_part = contract_last(dlatent_cols, w_in)
    d_win = lax.psum(win_part.astype(jnp.bfloat16), "grp").astype(jnp.float32)
    dpool = lax.psum(pool_part.astype(jnp.bfloat16), "seq").astype(jnp.float32) / lens_f
    denc = jnp.dot(member.astype(jnp.float32).T, dpool, precision=lax.Precision.HIGHEST)
    enc_part = jnp.sum(denc * unit, axis=0)
    scaled_e = denc * enc_gain
    dembedded = enc_rms * (scaled_e - unit * jnp.mean(scaled_e * unit, axis=-1, keepdims=True))
    table_part = jnp.dot(
        onehot_ids.astype(jnp.float32).T, dembedded, precision=lax.Precision.HIGHEST
    )
    d_emb, d_enc, d_lat = lax.psum((table_part, enc_part, lat_part), ("grp", "seq"))
    patch_out = patch_rows.reshape(1, 1, per_owner, patch_rows.shape[1])
    return (patch_out, d_emb, d_enc, d_win, d_lat, d_wg, d_wu, d_wd)


def solution(mesh):
    return jax.shard_map(
        on_device,
        mesh=mesh,
        in_specs=(
            P("grp", "seq"),
            P("grp", None),
            P("grp", None),
            P(),
            P(),
            P(None, "seq"),
            P(),
            P(("grp", "seq"), None),
            P(("grp", "seq"), None),
            P(("grp", "seq"), None),
            P("grp", "seq", None, None),
        ),
        out_specs=(
            P("grp", "seq", None, None),
            P(),
            P(),
            P(None, "seq"),
            P(),
            P(("grp", "seq"), None),
            P(("grp", "seq"), None),
            P(("grp", "seq"), None),
        ),
        check_vma=False,
    )
```

profile of v0, /device:TPU:1, one launch (start us, length us, event | category | flops | bytes accessed | tf_op | source)
XLA Modules:
  0.0 1998.8 jit_solution(14224874212962532686)
XLA Ops:
  7.2 0.0 all-reduce.6.cloned.1.call-start
  7.2 1.0 reduce-window.19
  8.3 0.1 slice.15
  8.4 0.1 slice_reduce_fusion.1
  8.5 0.1 broadcast_add_fusion
  8.6 0.7 sub.17
  9.3 0.7 fusion.49
  10.0 0.6 reduce-window.15
  10.5 0.2 slice_reduce_fusion
  10.8 0.8 fusion.48
  11.6 0.7 multiply_add_fusion
  12.2 1.4 multiply_reduce_fusion.2
  13.7 0.8 select_reduce_fusion
  14.5 2.0 fusion.16
  16.6 0.0 all-reduce.6.cloned.1.call-update
  16.6 0.0 all-gather.5.cloned.1.call-start
  16.6 108.2 %all-reduce.6.cloned.1.call-done = f32[256,1024]{1,0:T(8,128)} async-done(((f32[256,1024]{1,0:T(8,128)}), f32[256,1024]{1,0:T(8,128)}) %all-reduce.6.cloned.1.call-update) | async-done | bytes 1048592 | tf_op jit(solution)/shard_map/psum | solution.py:93
  124.9 1.4 divide_convert_fusion
  126.2 1.9 convolution_convert_fusion.2
  128.1 0.0 all-gather.5.cloned.1.call-update
  128.1 0.0 all-gather.7.cloned.1.call-start
  128.2 45.2 %all-gather.5.cloned.1.call-done = bf16[256,4096]{1,0:T(8,128)(2,1)} async-done(((bf16[256,128]{1,0:T(8,128)(2,1)}), bf16[256,4096]{1,0:T(8,128)(2,1)}) %all-gather.5.cloned.1.call-update) | async-done | bytes 2097168 | tf_op jit(solution)/shard_map/all_gather | solution.py:97
  173.3 0.0 all-gather.7.cloned.1.call-update
  173.4 0.0 all-gather.9.cloned.1.call-start
  173.4 0.5 all-gather.9.cloned.1.call-update
  173.9 0.0 reduce-scatter.5.cloned.1.call-start
  174.0 83.2 %all-gather.7.cloned.1.call-done = bf16[1024,4096]{1,0:T(8,128)(2,1)} async-done(((bf16[256,4096]{1,0:T(8,128)(2,1)}), bf16[1024,4096]{1,0:T(8,128)(2,1)}) %all-gather.7.cloned.1.call-update) | async-done | bytes 8388624 | tf_op jit(solution)/shard_map/all_gather | solution.py:102
  257.2 5.1 fusion
  262.3 10.4 fusion.2
  272.7 6.4 fusion.52
  279.1 3.6 fusion.51
  282.7 49.3 %all-gather.9.cloned.1.call-done = bf16[1,1,1024,4096]{3,2,1,0:T(8,128)(2,1)} async-done(((bf16[1,1,8,4096]{3,2,1,0:T(8,128)(2,1)}), bf16[1,1,1024,4096]{3,2,1,0:T(8,128)(2,1)}) %all-gather.9.cloned.1.call-update) | async-done | bytes 8388624 | tf_op jit(solution)/shard_map/all_gather | solution.py:110
  332.0 6.4 multiply_convert_fusion.1
  338.4 2.6 fusion.54
  341.0 9.3 convolution_add_fusion
  350.3 0.0 reduce-scatter.5.cloned.1.call-update
  350.3 0.0 reduce-scatter.3.cloned.1.call-start
  350.4 8.1 fusion.53
  358.4 0.0 reduce-scatter.3.cloned.1.call-update
  358.5 1.0 fusion.32
  359.5 648.1 %reduce-scatter.5.cloned.1.call-done = f32[8,4096]{1,0:T(8,128)} async-done(((f32[1024,4096]{1,0:T(8,128)}), f32[8,4096]{1,0:T(8,128)}) %reduce-scatter.5.cloned.1.call-update) | async-done | bytes 131088 | tf_op jit(solution)/shard_map/reduce_scatter | solution.py:114
  1007.6 1.1 fusion.30
  1008.8 661.9 %reduce-scatter.3.cloned.1.call-done = f32[8,4096]{1,0:T(8,128)} async-done(((f32[1024,4096]{1,0:T(8,128)}), f32[8,4096]{1,0:T(8,128)}) %reduce-scatter.3.cloned.1.call-update) | async-done | bytes 131088 | tf_op jit(solution)/shard_map/reduce_scatter | solution.py:104
  1670.6 1.7 fusion.35
  1672.4 10.2 all-to-all-start
  1682.6 0.0 all-reduce.8.cloned.1.call-start
  1682.7 6.0 fusion.56
  1688.6 1.4 all-to-all-done
  1690.1 1.1 convolution_convert_fusion
  1691.2 0.0 all-reduce.8.cloned.1.call-update
  1691.2 0.0 all-reduce.12.cloned.1.call-start
  1691.2 6.0 fusion.55
  1697.2 1.1 convolution_convert_fusion.1
  1698.3 0.0 all-reduce.12.cloned.1.call-update
  1698.3 0.3 all-reduce.10.cloned.1.call-start
  1698.6 93.7 %all-reduce.8.cloned.1.call-done = bf16[256,1024]{1,0:T(8,128)(2,1)} async-done(((bf16[256,1024]{1,0:T(8,128)(2,1)}), bf16[256,1024]{1,0:T(8,128)(2,1)}) %all-reduce.8.cloned.1.call-update) | async-done | bytes 524304 | tf_op jit(solution)/shard_map/psum | solution.py:134
  1792.3 1.9 multiply_reduce_fusion
  1794.2 1.8 fusion.8
  1796.0 6.0 fusion.3
  1801.9 31.8 %all-reduce.12.cloned.1.call-done = bf16[1024,128]{1,0:T(8,128)(2,1)} async-done(((bf16[1024,128]{1,0:T(8,128)(2,1)}), bf16[1024,128]{1,0:T(8,128)(2,1)}) %all-reduce.12.cloned.1.call-update) | async-done | bytes 262160 | tf_op jit(solution)/shard_map/psum | solution.py:133
  1833.7 1.8 convert_element_type.85
  1835.5 67.0 %all-reduce = (f32[1024]{0:T(1024)}, f32[4096]{0:T(1024)}) all-reduce(f32[1024]{0:T(1024)S(1)} %get-tuple-element.10, f32[4096]{0:T(1024)S(1)} %get-tuple-element.8), channel_id=1, replica_groups=mesh['grp'=4,'seq'=32] {'grp','seq'}, use_global_device_ids=true, to_apply=%region_18.19 | all-reduce | flops 5120 | bytes 40960 | tf_op jit(solution)/shard_map/psum | solution.py:142
  1902.5 87.5 %all-reduce.10.cloned.1.call-done = f32[256,1024]{1,0:T(8,128)} async-done(((f32[256,1024]{1,0:T(8,128)}), f32[256,1024]{1,0:T(8,128)}) %all-reduce.10.cloned.1.call-update) | async-done | bytes 1048592 | tf_op jit(solution)/shard_map/psum | solution.py:142
  1990.0 2.3 copy.27
  (31 shorter events, 0.2 us)
Async XLA Ops:
  7.2 324.8 %copy-start = (bf16[112,4096]{1,0:T(8,128)(2,1)S(1)}, bf16[112,4096]{1,0:T(8,128)(2,1)}, u32[]{:S(2)}) copy-start(bf16[112,4096]{1,0:T(8,128)(2,1)} %param.20) | copy-start | bytes 2752516
  7.2 117.7 %all-reduce.6.cloned.1.call-start = ((), (), s32[]{:S(2)}) async-start(), calls=%async_computation.3 | async-start | bytes 2097152 | tf_op jit(solution)/shard_map/psum | solution.py:93
  11.5 250.7 %copy-start.7 = (f32[4096]{0:T(1024)S(1)}, f32[4096]{0:T(1024)}, u32[]{:S(2)}) copy-start(f32[4096]{0:T(1024)} %param.17) | copy-start | bytes 49156
  16.6 156.8 %all-gather.5.cloned.1.call-start = ((), (), s32[]{:S(2)}) async-start(), calls=%async_computation.4 | async-start | bytes 2162688 | tf_op jit(solution)/shard_map/all_gather | solution.py:97
  128.1 129.0 %all-gather.7.cloned.1.call-start = ((), (), s32[]{:S(2)}) async-start(), calls=%async_computation.5 | async-start | bytes 10485760 | tf_op jit(solution)/shard_map/all_gather | solution.py:102
  173.4 158.6 %all-gather.9.cloned.1.call-start = ((), (), s32[]{:S(2)}) async-start(), calls=%async_computation.11 | async-start | bytes 8454144 | tf_op jit(solution)/shard_map/all_gather | solution.py:110
  173.9 833.7 %reduce-scatter.5.cloned.1.call-start = ((), (), s32[]{:S(2)}) async-start(), calls=%async_computation.7 | async-start | bytes 16908288 | tf_op jit(solution)/shard_map/reduce_scatter | solution.py:114
  262.3 10.4 copy-start.3
  272.7 6.4 copy-start.1
  272.7 6.4 copy-start.4
  332.0 6.4 copy-start.5
  350.3 1320.3 %reduce-scatter.3.cloned.1.call-start = ((), (), s32[]{:S(2)}) async-start(), calls=%async_computation.6 | async-start | bytes 16908288 | tf_op jit(solution)/shard_map/reduce_scatter | solution.py:104
  358.4 1312.2 %copy-start.6 = (bf16[1,1,8,4096]{3,2,1,0:T(8,128)(2,1)S(1)}, bf16[1,1,8,4096]{3,2,1,0:T(8,128)(2,1)}, u32[]{:S(2)}) copy-start(bf16[1,1,8,4096]{3,2,1,0:T(8,128)(2,1)} %param.21) | copy-start | bytes 196612
  358.5 1331.6 %copy-start.2 = (bf16[1024,128]{1,0:T(8,128)(2,1)S(1)}, bf16[1024,128]{1,0:T(8,128)(2,1)}, u32[]{:S(2)}) copy-start(bf16[1024,128]{1,0:T(8,128)(2,1)} %param.16) | copy-start | bytes 786436
  1672.4 17.7 all-to-all-start
  1682.6 109.7 %all-reduce.8.cloned.1.call-start = ((), (), s32[]{:S(2)}) async-start(), calls=%async_computation.8 | async-start | bytes 1048576 | tf_op jit(solution)/shard_map/psum | solution.py:134
  1691.1 101.2 %copy-start.8 = (f32[1024]{0:T(1024)S(1)}, f32[1024]{0:T(1024)}, u32[]{:S(2)}) copy-start(f32[1024]{0:T(1024)} %param.15) | copy-start | bytes 12292
  1691.2 103.0 %copy-start.9 = (s32[1,128]{1,0:T(1,128)S(1)}, s32[1,128]{1,0:T(1,128)}, u32[]{:S(2)}) copy-start(s32[1,128]{1,0:T(1,128)} %param.11) | copy-start | bytes 1540
  1691.2 142.5 %all-reduce.12.cloned.1.call-start = ((), (), s32[]{:S(2)}) async-start(), calls=%async_computation.10 | async-start | bytes 524288 | tf_op jit(solution)/shard_map/psum | solution.py:133
  1698.3 291.7 %all-reduce.10.cloned.1.call-start = ((), (), s32[]{:S(2)}) async-start(), calls=%async_computation.9 | async-start | bytes 2097152 | tf_op jit(solution)/shard_map/psum | solution.py:142
Sparse Core Ops, SparseCore 0:
  16.7 108.1 all-reduce.5
  128.3 45.0 all-gather.4
  175.1 82.0 all-gather.6
  260.5 71.5 all-gather.8
  350.4 657.1 reduce-scatter.4
  1010.0 660.5 reduce-scatter.2
  1691.3 100.9 all-reduce.7
  1794.6 39.0 all-reduce.11
  1839.8 150.1 all-reduce.9
where the time goes:
time: 2000 us
  waiting for transfers between devices  1810 us (90%)
  blocking collectives  67 us (3%)
  matrix products  65.3 us (3%)
  other arithmetic  28 us (1%)
    reduce_scatter x1, waiting for transfers between devices, on_device(): lax.psum_scatter(jnp.dot(hidden, w_down, preferred_element_type=jnp.float...  662 us
    reduce_scatter x1, waiting for transfers between devices, on_device(): lax.psum_scatter(jnp.dot(dgate, w_gate, preferred_element_type=jnp.float3...  648 us
    psum x1, waiting for transfers between devices, on_device(): pooled_sum = lax.psum(partial_pool, 'seq')  108 us
    psum x1, waiting for transfers between devices, on_device(): lax.psum(pool_part.astype(jnp.bfloat16), 'seq').astype(jnp.float32) / lens_f  93.7 us
    psum x1, waiting for transfers between devices, on_device(): lax.psum((table_part, enc_part, lat_part), ('grp', 'seq'))  87.5 us
    all_gather x1, waiting for transfers between devices, on_device(): rows = lax.all_gather(latent, 'grp', axis=0, tiled=True)  83.2 us
    psum x1, blocking collectives, on_device(): lax.psum((table_part, enc_part, lat_part), ('grp', 'seq'))  67 us
    all_gather x1, waiting for transfers between devices, on_device(): cot_all = lax.all_gather(cot_own, ('grp', 'seq'), axis=0, tiled=True)  49.3 us
  transfers between devices with their start and end apart: 10, of which 10 were waited for; matrix products, arithmetic and copies ran while one was open for 3% of the time, Pallas kernels for 0%

commit v1 on v0

v1 whole, which is shorter than its diff:
```python
import jax
import jax.numpy as jnp
from jax import lax
from jax.sharding import Mesh, PartitionSpec as P

CHIPS = ("y", "z", "x")
ALL = ("y", "z", "x", "c")
bf16 = jnp.bfloat16
f32 = jnp.float32


def rms_scale(values):
    return lax.rsqrt(jnp.mean(values * values, axis=-1, keepdims=True) + 1e-05)


def silu_parts(gate):
    sigma = jax.nn.sigmoid(gate)
    return (gate * sigma, sigma * (1.0 + gate * (1.0 - sigma)))


def owner_slots(lengths, owners, owner_count, per_owner):
    count = lengths.shape[0]
    onehot_own = (owners[:, None] == jnp.arange(owner_count, dtype=jnp.int32)[None, :]).astype(
        jnp.int32
    )
    rank = jnp.sum((jnp.cumsum(onehot_own, axis=0) - onehot_own) * onehot_own, axis=1)
    target = owners * per_owner + rank
    placed = target[None, :] == jnp.arange(count, dtype=jnp.int32)[:, None]
    starts = jnp.cumsum(lengths) - lengths
    slot_start = jnp.sum(jnp.where(placed, starts[None, :], 0), axis=1)
    slot_len = jnp.sum(jnp.where(placed, lengths[None, :], 0), axis=1)
    return (slot_start, slot_len)


def contract_last(left, right):
    return lax.dot_general(
        left, right, (((1,), (1,)), ((), ())), preferred_element_type=f32
    )


def contract_first(left, right):
    return lax.dot_general(
        left, right, (((0,), (0,)), ((), ())), preferred_element_type=f32
    )


def slot_counts(ids, lengths, owners, vocab):
    slot_start, slot_len = owner_slots(lengths, owners, 32, 8)
    position = jnp.arange(ids.shape[0], dtype=jnp.int32)
    member = (position[None, :] >= slot_start[:, None]) & (
        position[None, :] < (slot_start + slot_len)[:, None]
    )
    onehot = ids[:, None] == jnp.arange(vocab, dtype=jnp.int32)[None, :]
    counts = jnp.dot(member.astype(bf16), onehot.astype(bf16), preferred_element_type=f32)
    return counts, slot_len


def reduce_rows(left, right, core):
    rows = left.reshape(64, 2, 8, left.shape[1])
    other = lax.dynamic_index_in_dim(rows, 1 - core, 1, keepdims=False).reshape(512, -1)
    own = lax.dynamic_index_in_dim(rows, core, 1, keepdims=False).reshape(512, -1)
    away = jnp.dot(other, right, preferred_element_type=f32).astype(bf16)
    came = lax.ppermute(away, "c", [(0, 1), (1, 0)])
    here = (jnp.dot(own, right, preferred_element_type=f32) + came.astype(f32)).astype(bf16)
    parts = lax.all_to_all(here.reshape(64, 8, -1), CHIPS, 0, 0, tiled=True)
    return jnp.sum(parts.astype(f32), axis=0)


def on_device(
    byte_ids, patch_lengths, patch_owner, emb_table, enc_gain, w_in, lat_gain,
    w_gate, w_up, w_down, grad_out,
):
    y = lax.axis_index("y")
    core = lax.axis_index("c")
    seq = lax.axis_index(("z", "x", "c"))
    vocab, width = emb_table.shape
    latd = lat_gain.shape[0]
    cot_own = grad_out[0, 0]

    tiny = jnp.concatenate(
        [
            byte_ids[0],
            lax.dynamic_slice_in_dim(patch_lengths[0], seq * 8, 8),
            lax.dynamic_slice_in_dim(patch_owner[0], seq * 8, 8),
            jnp.zeros((112,), jnp.int32),
        ]
    )
    win_quarter = lax.dynamic_slice_in_dim(w_in, y * 256, 256, 0)
    mine = jnp.concatenate([cot_own, win_quarter.reshape(8, latd)], axis=0)
    whole = lax.all_gather(mine[None], ALL, axis=0, tiled=True)
    tiny_all = lax.all_gather(tiny[None], ALL, axis=0, tiled=True)
    ids = tiny_all[:, :128].reshape(4, 4096)
    lengths = tiny_all[:, 128:136].reshape(4, 256)
    owners = tiny_all[:, 136:144].reshape(4, 256)

    embedded = emb_table.astype(f32)
    enc_rms = rms_scale(embedded)
    unit = embedded * enc_rms
    table = (unit * enc_gain).astype(bf16)
    counts, slot_len = jax.vmap(lambda i, n, o: slot_counts(i, n, o, vocab))(ids, lengths, owners)
    counts = counts.reshape(1024, vocab)
    lens = slot_len.reshape(1024, 1).astype(f32)
    pooled = (jnp.dot(counts.astype(bf16), table, preferred_element_type=f32) / lens).astype(bf16)

    cot_all = whole[:, :8].reshape(1024, latd)
    win_all = (
        whole[:, 8:].reshape(4, 32, 256, 128).transpose(0, 2, 1, 3).reshape(1024, latd)
    )
    latent = jnp.dot(pooled, win_all, preferred_element_type=f32).astype(bf16)

    lat32 = latent.astype(f32)
    normed = (lat32 * rms_scale(lat32) * lat_gain).astype(bf16)
    gate = contract_last(normed, w_gate)
    upper = contract_last(normed, w_up)
    active, slope = silu_parts(gate)
    hidden = (active * upper).astype(bf16)
    dhid = contract_last(cot_all, w_down)
    dgate = (dhid * upper * slope).astype(bf16)
    dup = (dhid * active).astype(bf16)

    dnormed = reduce_rows(
        jnp.concatenate([dgate, dup], axis=1), jnp.concatenate([w_gate, w_up], axis=0), core
    )
    mlp_own = reduce_rows(hidden, w_down, core)
    d_wd = contract_first(hidden, cot_all)
    d_wg = contract_first(dgate, normed)
    d_wu = contract_first(dup, normed)

    row0 = y * 256 + seq * 8
    own_lat = lax.dynamic_slice_in_dim(latent, row0, 8, 0).astype(f32)
    lat_rms = rms_scale(own_lat)
    unit_l = own_lat * lat_rms
    lat_part = jnp.sum(dnormed * unit_l, axis=0, keepdims=True)
    scaled = dnormed * lat_gain
    dlatent = (
        cot_own.astype(f32)
        + lat_rms * (scaled - unit_l * jnp.mean(scaled * unit_l, axis=-1, keepdims=True))
    ).astype(bf16)
    own_counts = lax.dynamic_slice_in_dim(counts, row0, 8, 0)
    own_len = lax.dynamic_slice_in_dim(lens, row0, 8, 0)
    dpool = contract_last(dlatent, win_all) / own_len
    value_part = lax.dot_general(
        own_counts, dpool, (((0,), (0,)), ((), ())), precision=lax.Precision.HIGHEST,
        preferred_element_type=f32,
    ).astype(bf16)

    columns = jnp.concatenate([dlatent, lat_part.astype(bf16)], axis=0)
    columns = columns.reshape(9, 32, 128).transpose(1, 0, 2)
    columns = jnp.broadcast_to(columns[None], (4, 32, 9, 128)).reshape(128, 9, 128)
    sent = jnp.concatenate([columns, value_part.reshape(128, 16, 128)], axis=1)
    got = lax.all_to_all(sent, ALL, 0, 0, tiled=True)
    dlat_cols = got[:, :8].reshape(1024, 128)
    d_lat_cols = jnp.sum(got[:, 8].astype(f32), axis=0)
    values = jnp.sum(got[:, 9:].astype(f32), axis=0).reshape(2, width)
    d_win = contract_first(pooled, dlat_cols)

    value0 = (y * 32 + seq) * 2
    my_unit = lax.dynamic_slice_in_dim(unit, value0, 2, 0)
    my_rms = lax.dynamic_slice_in_dim(enc_rms, value0, 2, 0)
    enc_part = jnp.sum(values * my_unit, axis=0)
    scaled_e = values * enc_gain
    d_rows = my_rms * (scaled_e - my_unit * jnp.mean(scaled_e * my_unit, axis=-1, keepdims=True))
    last = jnp.concatenate(
        [d_rows.reshape(-1), enc_part, d_lat_cols, jnp.zeros((896,), f32)]
    ).astype(bf16)
    last = jnp.broadcast_to(last.reshape(1, 32, 128), (128, 32, 128))
    ends = lax.all_to_all(last, ALL, 0, 0, tiled=True)
    d_emb = ends[:, :16].reshape(vocab, width).astype(f32)
    d_enc = jnp.sum(ends[:, 16:24].astype(f32), axis=0).reshape(width)
    d_lat = ends[:32, 24].reshape(latd).astype(f32)

    patch_out = (own_lat + mlp_own).astype(bf16).reshape(1, 1, 8, latd)
    return (patch_out, d_emb, d_enc, d_win, d_lat, d_wg, d_wu, d_wd)


def solution(mesh):
    fine = Mesh(mesh.devices.reshape(4, 4, 4, 2), ALL)
    seq = ("z", "x", "c")
    ff = P(ALL, None)
    return jax.shard_map(
        on_device,
        mesh=fine,
        in_specs=(
            P("y", seq), P("y", None), P("y", None), P(), P(), P(None, seq), P(),
            ff, ff, ff, P("y", seq, None, None),
        ),
        out_specs=(P("y", seq, None, None), P(), P(), P(None, seq), P(), ff, ff, ff),
        check_vma=False,
    )
```

time: 2000 us -> 398 us (0.20)
  waiting for transfers between devices: 1810 us -> 139 us
  local copies, waits for them, and re-layouts: 2.74 us -> 46.4 us
  blocking collectives: 67 us -> 38.7 us
  matrix products: 65.3 us -> 86.2 us
    reduce_scatter x2 -> x0, waiting for transfers between devices: 1310 us -> none  [the longest x1 662 us: on_device(): lax.psum_scatter(jnp.dot(hidden, w_down, preferred_element_type=jnp.float...]
    psum x4 -> x0, waiting for transfers between devices: 321 us -> none  [the longest x1 108 us: on_device(): pooled_sum = lax.psum(partial_pool, 'seq')]
    all_gather x3 -> x1, waiting for transfers between devices: 178 us -> 23.8 us  [on_device(): whole = lax.all_gather(mine[None], ALL, axis=0, tiled=True)]
    all_to_all x1 -> x4, waiting for transfers between devices: 1.43 us -> 114 us  [the longest x2 96 us: reduce_rows(): parts = lax.all_to_all(here.reshape(64, 8, -1), CHIPS, 0, 0, tiled=True)]
    psum x1 -> x0, blocking collectives: 67 us -> none  [on_device(): lax.psum((table_part, enc_part, lat_part), ('grp', 'seq'))]
    all_gather x0 -> x1, blocking collectives: none -> 38.7 us  [on_device(): tiny_all = lax.all_gather(tiny[None], ALL, axis=0, tiled=True)]
  transfers between devices with their start and end apart: 10 -> 7, of which waited for: 10 -> 6; matrix products, arithmetic and copies ran while one was open for 3% -> 17% of each run, Pallas kernels for 0% -> 0%
where the time goes in v1:
time: 398 us; the launch traced here: 391 us
  waiting for transfers between devices  139 us (35%)
  matrix products  86.2 us (22%)
  local copies, waits for them, and re-layouts  46.4 us (12%)
  other arithmetic  38.9 us (10%)
  blocking collectives  38.7 us (10%)
  starting transfers between devices  27 us (7%)
  between operations  14.8 us (4%)
    all_to_all x2, waiting for transfers between devices, reduce_rows(): parts = lax.all_to_all(here.reshape(64, 8, -1), CHIPS, 0, 0, tiled=True)  96 us
    all_gather x1, blocking collectives, on_device(): tiny_all = lax.all_gather(tiny[None], ALL, axis=0, tiled=True)  38.7 us
    dot_general x4, matrix products, contract_last(): lax.dot_general(left, right, (((1,), (1,)), ((), ())), preferred_element_...  24.6 us
    all_gather x1, waiting for transfers between devices, on_device(): whole = lax.all_gather(mine[None], ALL, axis=0, tiled=True)  23.8 us
    dot_general x4, matrix products, contract_first(): lax.dot_general(left, right, (((0,), (0,)), ((), ())), preferred_element_...  19.6 us
    dot_general x1, matrix products, on_device(): latent = jnp.dot(pooled, win_all, preferred_element_type=f32).astype(bf16)  14.8 us
    all_to_all x2, starting transfers between devices, reduce_rows(): parts = lax.all_to_all(here.reshape(64, 8, -1), CHIPS, 0, 0, tiled=True)  14.6 us
    reshape x1, local copies, waits for them, and re-layouts, on_device(): whole[:, 8:].reshape(4, 32, 256, 128).transpose(0, 2, 1, 3)  13.9 us
  transfers between devices with their start and end apart: 7, of which 6 were waited for; matrix products, arithmetic and copies ran while one was open for 17% of the time, Pallas kernels for 0%

profile of v1, /device:TPU:1, one launch (start us, length us, event | category | flops | bytes accessed | tf_op | source)
XLA Modules:
  0.0 390.8 jit_solution(17461751072436554975)
XLA Ops:
  7.2 0.9 constant_dynamic-slice_fusion.1
  8.2 1.5 pad_maximum_fusion.2
  9.7 0.7 fusion.69
  10.5 0.7 pad_add_fusion
  11.2 38.7 %all-gather.2 = s32[128,1,256]{2,1,0:T(1,128)S(1)} all-gather(s32[1,1,256]{2,1,0:T(1,128)S(1)} %bitcast.149), channel_id=2, replica_groups=mesh['y'=4,'z'=4,'x'=4,'c'=2] {'y','z','x','c'}, dimensions={0}, use_global_device_ids=true | all-gather | bytes 132096 | tf_op jit(solution)/shard_map/all_gather | solution.py:91
  50.4 1.2 reduce-window.16
  52.0 2.3 reduce-window.14
  54.7 0.4 select_reduce_fusion.1
  55.2 1.2 fusion.25
  56.4 1.2 constant_dynamic-update-slice_fusion.1
  57.7 1.2 constant_dynamic-update-slice_fusion
  58.9 4.8 %fusion.97 = pred[4,256,4096]{2,1,0:T(32,128)(4,1)S(1)} fusion(s32[4,256]{1,0:T(4,128)S(1)} %get-tuple-element.23, s32[4,256]{1,0:T(4,128)S(1)} %get-tuple-element.12), kind=kLoop, calls=%fused_computation.8.clone.clone.2 | loop fusion | flops 12582912 | bytes 4202496 | tf_op jit(solution)/shard_map/vmap()/dot_general | solution.py:54
  63.7 4.9 %fusion.4 = f32[4,256,256]{2,1,0:T(8,128)S(1)} fusion(s32[4,4096]{1,0:T(4,128)S(1)} %eq.61, pred[4,256,4096]{2,1,0:T(32,128)(4,1)S(1)} %fusion.97), kind=kOutput, calls=%fused_computation.9 | convolution fusion | flops 2151677952 | bytes 5308416 | tf_op jit(solution)/shard_map/vmap()/dot_general | solution.py:54
  68.7 1.0 copy-done.14
  69.7 2.2 divide_convert_fusion
  71.9 23.8 %all-gather.5.cloned.1.call-done = bf16[2048,4096]{1,0:T(8,128)(2,1)} async-done(((bf16[16,4096]{1,0:T(8,128)(2,1)}), bf16[2048,4096]{1,0:T(8,128)(2,1)}) %all-gather.5.cloned.1.call-update) | async-done | bytes 16777232 | tf_op jit(solution)/shard_map/all_gather | solution.py:90
  95.6 7.7 %slice.66 = bf16[128,8,4096]{2,1,0:T(8,128)(2,1)} slice(bf16[128,16,4096]{2,1,0:T(8,128)(2,1)} %bitcast.133), slice={[0:128], [8:16], [0:4096]} | slice | bytes 16777216 | tf_op jit(solution)/shard_map/slice | solution.py:107
  103.3 7.0 %fusion.17 = f32[1024,112]{0,1:T(8,128)} fusion(bf16[112,4096]{1,0:T(8,128)(2,1)S(1)} %copy-done, bf16[128,16,4096]{2,1,0:T(8,128)(2,1)} %bitcast.134), kind=kOutput, calls=%fused_computation.24 | convolution fusion | flops 939524096 | bytes 9764864 | tf_op jit(solution)/shard_map/dot_general | solution.py:36
  110.3 13.9 %reshape.244 = bf16[4,32,256,128]{3,2,1,0:T(8,128)(2,1)} reshape(bf16[128,8,4096]{2,1,0:T(8,128)(2,1)} %slice.66) | data formatting | bytes 16777216 | tf_op jit(solution)/shard_map/reshape | solution.py:107
  124.2 12.1 %copy.52 = bf16[4,256,32,128]{3,2,1,0:T(8,128)(2,1)} copy(bf16[4,256,32,128]{3,1,2,0:T(8,128)(2,1)} %bitcast.132) | data formatting | bytes 16777216 | tf_op jit(solution)/shard_map/transpose | solution.py:107
  136.4 14.8 %fusion = (f32[1024]{0:T(1024)S(1)}, bf16[1024,4096]{1,0:T(8,128)(2,1)}) fusion(bf16[1024,1024]{1,0:T(8,128)(2,1)S(1)} %copy-done.2, bf16[128,8,32,128]{3,2,1,0:T(8,128)(2,1)} %bitcast.130), kind=kOutput, calls=%fused_computation.2 | convolution fusion | flops 8606710784 | bytes 18878464 | tf_op jit(solution)/shard_map/dot_general | solution.py:109
  151.2 10.4 %fusion.2 = bf16[1024,4096]{1,0:T(8,128)(2,1)} fusion(bf16[1024,4096]{1,0:T(8,128)(2,1)} %get-tuple-element.25, f32[4096]{0:T(1024)S(1)} %copy-done.12, f32[1024]{0:T(1024)S(1)} %add_rsqrt_fusion), kind=kLoop, calls=%fused_computation.4 | loop fusion | flops 16777216 | bytes 16797696 | tf_op jit(solution)/shard_map/convert_element_type | solution.py:112
  161.6 6.4 %fusion.73 = f32[1024,112]{0,1:T(8,128)S(1)} fusion(bf16[1024,4096]{1,0:T(8,128)(2,1)} %fusion.2, bf16[112,4096]{1,0:T(8,128)(2,1)S(1)} %copy-done.8), kind=kOutput, calls=%fused_computation.129 | convolution fusion | flops 939524096 | bytes 9764864 | tf_op jit(solution)/shard_map/dot_general | solution.py:36
  168.0 3.7 multiply_convert_fusion.3
  171.7 0.7 copy-done.6
  172.4 0.8 pad_maximum_fusion.1
  173.2 1.2 copy.54
  174.5 3.3 convolution_convert_fusion
  177.7 0.3 collective-permute-start.1
  178.0 1.8 copy.53
  179.8 4.1 %convolution_convert_fusion.1 = bf16[512,4096]{1,0:T(8,128)(2,1)} fusion(bf16[112,4096]{1,0:T(8,128)(2,1)S(1)} %copy-done, bf16[64,2,8,112]{3,2,1,0:T(8,128)(2,1)} %bitcast.139, s32[]{:T(128)S(6)} %select_n.39), kind=kOutput, calls=%fused_computation.28 | convolution fusion | flops 471859200 | bytes 5242884 | tf_op jit(solution)/shard_map/dot_general | solution.py:62
  183.9 0.4 collective-permute-start
  184.3 0.9 collective-permute-done.1
  185.2 5.5 %fusion.21 = bf16[64,8,4096]{2,1,0:T(8,128)(2,1)} fusion(bf16[512,4096]{1,0:T(8,128)(2,1)} %collective-permute-done.1, bf16[224,4096]{1,0:T(8,128)(2,1)S(1)} %constant_dynamic-update-slice_fusion, bf16[64,2,8,224]{3,2,1,0:T(8,128)(2,1)S(1)} %bitcast.137, s32[]{:T(128)S(6)} %select_n.38), kind=kOutput, calls=%fused_computation.30 | convolution fusion | flops 945815552 | bytes 10485764 | tf_op jit(solution)/shard_map/dot_general | solution.py:64
  190.8 8.5 %all-to-all-start.1 = ((bf16[64,8,4096]{2,1,0:T(8,128)(2,1)}), bf16[64,8,4096]{2,1,0:T(8,128)(2,1)}, u32[]{:S(2)}, u32[]{:S(2)}) async-start(bf16[64,8,4096]{2,1,0:T(8,128)(2,1)} %fusion.21), calls=%async_computation.1 | async-start | bytes 8388608 | tf_op jit(solution)/shard_map/all_to_all | solution.py:65
  199.3 5.5 %fusion.20 = bf16[64,8,4096]{2,1,0:T(8,128)(2,1)} fusion(bf16[512,4096]{1,0:T(8,128)(2,1)} %collective-permute-done, bf16[112,4096]{1,0:T(8,128)(2,1)S(1)} %copy-done, bf16[64,2,8,112]{3,2,1,0:T(8,128)(2,1)} %bitcast.140, s32[]{:T(128)S(6)} %select_n.38), kind=kOutput, calls=%fused_computation.29 | convolution fusion | flops 476053504 | bytes 9437188 | tf_op jit(solution)/shard_map/dot_general | solution.py:64
  204.8 48.4 %all-to-all-done.1 = bf16[64,8,4096]{2,1,0:T(8,128)(2,1)} async-done(((bf16[64,8,4096]{2,1,0:T(8,128)(2,1)}), bf16[64,8,4096]{2,1,0:T(8,128)(2,1)}, u32[]{:S(2)}, u32[]{:S(2)}) %all-to-all-start.1) | async-done | bytes 4194336 | tf_op jit(solution)/shard_map/all_to_all | solution.py:65
  253.2 6.1 %all-to-all-start = ((bf16[64,8,4096]{2,1,0:T(8,128)(2,1)}), bf16[64,8,4096]{2,1,0:T(8,128)(2,1)}, u32[]{:S(2)}, u32[]{:S(2)}) async-start(bf16[64,8,4096]{2,1,0:T(8,128)(2,1)} %fusion.20), calls=%async_computation | async-start | bytes 8388608 | tf_op jit(solution)/shard_map/all_to_all | solution.py:65
  259.4 1.0 fusion.47
  260.4 2.8 convert_reduce_fusion
  263.2 1.1 fusion.45
  264.3 47.5 %all-to-all-done = bf16[64,8,4096]{2,1,0:T(8,128)(2,1)} async-done(((bf16[64,8,4096]{2,1,0:T(8,128)(2,1)}), bf16[64,8,4096]{2,1,0:T(8,128)(2,1)}, u32[]{:S(2)}, u32[]{:S(2)}) %all-to-all-start) | async-done | bytes 4194336 | tf_op jit(solution)/shard_map/all_to_all | solution.py:65
  311.8 2.8 convert_reduce_fusion.1
  314.7 1.5 fusion.44
  316.2 7.6 %fusion.22 = f32[8,1024]{1,0:T(8,128)S(1)} fusion(bf16[8,4096]{1,0:T(8,128)(2,1)S(1)} %get-tuple-element.14, bf16[128,8,32,128]{3,2,1,0:T(8,128)(2,1)} %bitcast.131, f32[8]{0:T(128)S(1)} %fusion.71), kind=kOutput, calls=%fused_computation.35 | convolution fusion | flops 67117056 | bytes 8486944 | tf_op jit(solution)/shard_map/dot_general | solution.py:36
  323.8 1.7 convolution_convert_fusion.2
  325.5 0.2 reshape.257
  325.9 1.3 pad_maximum_fusion
  327.2 7.2 %all-to-all-start.2 = ((bf16[128,25,128]{2,1,0:T(8,128)(2,1)}), bf16[128,25,128]{2,1,0:T(8,128)(2,1)S(1)}, u32[]{:S(2)}, u32[]{:S(2)}) async-start(bf16[128,25,128]{2,1,0:T(8,128)(2,1)} %pad_maximum_fusion), calls=%async_computation.2 | async-start | bytes 2097152 | tf_op jit(solution)/shard_map/all_to_all | solution.py:151
  334.5 1.1 convert_multiply_fusion.2
  335.6 6.0 %fusion.74 = f32[112,4096]{1,0:T(8,128)} fusion(bf16[1024,112]{0,1:T(8,128)(2,1)S(1)} %copy-done.7, bf16[1024,4096]{1,0:T(8,128)(2,1)} %fusion.2), kind=kOutput, calls=%fused_computation.130 | convolution fusion | flops 939524096 | bytes 10452992 | tf_op jit(solution)/shard_map/dot_general | solution.py:42
  341.6 12.2 %all-to-all-done.2 = bf16[128,25,128]{2,1,0:T(8,128)(2,1)S(1)} async-done(((bf16[128,25,128]{2,1,0:T(8,128)(2,1)}), bf16[128,25,128]{2,1,0:T(8,128)(2,1)S(1)}, u32[]{:S(2)}, u32[]{:S(2)}) %all-to-all-start.2) | async-done | bytes 819232 | tf_op jit(solution)/shard_map/all_to_all | solution.py:151
  353.8 0.2 convert_reduce_fusion.2
  354.0 0.9 multiply_reduce_fusion.1
  354.9 0.8 fusion.63
  355.9 1.1 broadcast_in_dim.68
  357.0 4.4 %all-to-all-start.3 = ((bf16[128,32,128]{2,1,0:T(8,128)(2,1)}), bf16[128,32,128]{2,1,0:T(8,128)(2,1)S(1)}, u32[]{:S(2)}, u32[]{:S(2)}) async-start(bf16[128,32,128]{2,1,0:T(8,128)(2,1)} %broadcast_in_dim.68), calls=%async_computation.3 | async-start | bytes 2097152 | tf_op jit(solution)/shard_map/all_to_all | solution.py:167
  361.5 6.0 %fusion.75 = f32[112,4096]{1,0:T(8,128)} fusion(bf16[1024,112]{0,1:T(8,128)(2,1)S(1)} %get-tuple-element.17, bf16[1024,4096]{1,0:T(8,128)(2,1)} %fusion.2), kind=kOutput, calls=%fused_computation.131 | convolution fusion | flops 939524096 | bytes 10452992 | tf_op jit(solution)/shard_map/dot_general | solution.py:42
  367.4 6.1 %fusion.16 = f32[112,4096]{1,0:T(8,128)} fusion(bf16[1024,112]{0,1:T(8,128)(2,1)S(1)} %copy-done.11, bf16[128,16,4096]{2,1,0:T(8,128)(2,1)} %bitcast.135), kind=kOutput, calls=%fused_computation.23 | convolution fusion | flops 939524096 | bytes 10452992 | tf_op jit(solution)/shard_map/dot_general | solution.py:42
  373.5 1.5 fusion.29
  375.1 5.9 %all-to-all-done.3 = bf16[128,32,128]{2,1,0:T(8,128)(2,1)S(1)} async-done(((bf16[128,32,128]{2,1,0:T(8,128)(2,1)}), bf16[128,32,128]{2,1,0:T(8,128)(2,1)S(1)}, u32[]{:S(2)}, u32[]{:S(2)}) %all-to-all-start.3) | async-done | bytes 1048608 | tf_op jit(solution)/shard_map/all_to_all | solution.py:167
  381.0 1.1 reshape.262
  382.2 0.7 convert_reduce_fusion.3
  382.9 0.6 slice_convert_fusion.1
  (77 shorter events, 2.0 us)
Async XLA Ops:
  7.2 96.2 %copy-start = (bf16[112,4096]{1,0:T(8,128)(2,1)S(1)}, bf16[112,4096]{1,0:T(8,128)(2,1)}, u32[]{:S(2)}) copy-start(bf16[112,4096]{1,0:T(8,128)(2,1)} %param.20) | copy-start | bytes 2752516
  7.2 88.4 %all-gather.5.cloned.1.call-start = ((), (), s32[]{:S(2)}) async-start(), calls=%async_computation.4 | async-start | bytes 16908288 | tf_op jit(solution)/shard_map/all_gather | solution.py:90
  63.7 5.9 %copy-start.4 = (bf16[256,1024]{1,0:T(8,128)(2,1)S(1)}, bf16[256,1024]{1,0:T(8,128)(2,1)}, u32[]{:S(2)}) copy-start(bf16[256,1024]{1,0:T(8,128)(2,1)} %param.14) | copy-start | bytes 1572868
  63.7 5.9 %copy-start.13 = (f32[1024]{0:T(1024)S(1)}, f32[1024]{0:T(1024)}, u32[]{:S(2)}) copy-start(f32[1024]{0:T(1024)} %param.15) | copy-start | bytes 12292
  68.7 1.0 copy-start.14
  124.2 12.2 %copy-start.2 = (bf16[1024,1024]{1,0:T(8,128)(2,1)S(1)}, bf16[1024,1024]{1,0:T(8,128)(2,1)}, u32[]{:S(2)}) copy-start(bf16[1024,1024]{1,0:T(8,128)(2,1)} %divide_convert_fusion) | copy-start | bytes 6291460
  136.4 14.8 %copy-start.12 = (f32[4096]{0:T(1024)S(1)}, f32[4096]{0:T(1024)}, u32[]{:S(2)}) copy-start(f32[4096]{0:T(1024)} %param.17) | copy-start | bytes 49156
  151.2 10.4 %copy-start.8 = (bf16[112,4096]{1,0:T(8,128)(2,1)S(1)}, bf16[112,4096]{1,0:T(8,128)(2,1)}, u32[]{:S(2)}) copy-start(bf16[112,4096]{1,0:T(8,128)(2,1)} %param.19) | copy-start | bytes 2752516
  161.6 6.4 %copy-start.1 = (bf16[1024,4096]{1,0:T(8,128)(2,1)S(1)}, bf16[1024,4096]{1,0:T(8,128)(2,1)}, u32[]{:S(2)}) copy-start(bf16[1024,4096]{1,0:T(8,128)(2,1)} %fusion.2) | copy-start | bytes 25165828
  161.6 6.4 %copy-start.9 = (bf16[112,4096]{1,0:T(8,128)(2,1)S(1)}, bf16[112,4096]{1,0:T(8,128)(2,1)}, u32[]{:S(2)}) copy-start(bf16[112,4096]{1,0:T(8,128)(2,1)} %param.18) | copy-start | bytes 2752516
  161.6 6.4 %copy-start.15 = (f32[1024,112]{0,1:T(8,128)S(1)}, f32[1024,112]{0,1:T(8,128)}, u32[]{:S(2)}) copy-start(f32[1024,112]{0,1:T(8,128)} %fusion.17) | copy-start | bytes 1376260
  171.7 0.7 copy-start.6
  177.7 7.5 %collective-permute-start.1 = (bf16[512,4096]{1,0:T(8,128)(2,1)}, bf16[512,4096]{1,0:T(8,128)(2,1)}, u32[]{:S(2)}, u32[]{:S(2)}) collective-permute-start(bf16[512,4096]{1,0:T(8,128)(2,1)} %convolution_convert_fusion), channel_id=1, source_target_pairs={{0,1},{1,0},{2,3},{3,2},{4,5},{5,4},{6,7},{7,6},{8,9},{9,8},{10,11... | collective-permute-start | bytes 12582920 | tf_op jit(solution)/shard_map/ppermute | solution.py:63
  183.9 15.4 %collective-permute-start = (bf16[512,4096]{1,0:T(8,128)(2,1)}, bf16[512,4096]{1,0:T(8,128)(2,1)}, u32[]{:S(2)}, u32[]{:S(2)}) collective-permute-start(bf16[512,4096]{1,0:T(8,128)(2,1)} %convolution_convert_fusion.1), channel_id=1, source_target_pairs={{0,1},{1,0},{2,3},{3,2},{4,5},{5,4},{6,7},{7,6},{8,9},{9,8},{10,11... | collective-permute-start | bytes 12582920 | tf_op jit(solution)/shard_map/ppermute | solution.py:63
  190.8 62.4 %all-to-all-start.1 = ((bf16[64,8,4096]{2,1,0:T(8,128)(2,1)}), bf16[64,8,4096]{2,1,0:T(8,128)(2,1)}, u32[]{:S(2)}, u32[]{:S(2)}) async-start(bf16[64,8,4096]{2,1,0:T(8,128)(2,1)} %fusion.21), calls=%async_computation.1 | async-start | bytes 8388608 | tf_op jit(solution)/shard_map/all_to_all | solution.py:65
  204.8 109.9 %copy-start.10 = (bf16[1,1,8,4096]{3,2,1,0:T(8,128)(2,1)S(1)}, bf16[1,1,8,4096]{3,2,1,0:T(8,128)(2,1)}, u32[]{:S(2)}) copy-start(bf16[1,1,8,4096]{3,2,1,0:T(8,128)(2,1)} %param.21) | copy-start | bytes 196612
  253.2 58.7 %all-to-all-start = ((bf16[64,8,4096]{2,1,0:T(8,128)(2,1)}), bf16[64,8,4096]{2,1,0:T(8,128)(2,1)}, u32[]{:S(2)}, u32[]{:S(2)}) async-start(bf16[64,8,4096]{2,1,0:T(8,128)(2,1)} %fusion.20), calls=%async_computation | async-start | bytes 8388608 | tf_op jit(solution)/shard_map/all_to_all | solution.py:65
  314.6 19.9 %copy-start.5 = (bf16[256,1024]{1,0:T(8,128)(2,1)S(1)}, bf16[256,1024]{1,0:T(8,128)(2,1)}, u32[]{:S(2)}) copy-start(bf16[256,1024]{1,0:T(8,128)(2,1)} %param.14) | copy-start | bytes 1572868
  316.2 19.4 %copy-start.7 = (bf16[1024,112]{0,1:T(8,128)(2,1)S(1)}, bf16[1024,112]{0,1:T(8,128)(2,1)}, u32[]{:S(2)}) copy-start(bf16[1024,112]{0,1:T(8,128)(2,1)} %copy-done.6) | copy-start | bytes 688132
  327.2 26.6 %all-to-all-start.2 = ((bf16[128,25,128]{2,1,0:T(8,128)(2,1)}), bf16[128,25,128]{2,1,0:T(8,128)(2,1)S(1)}, u32[]{:S(2)}, u32[]{:S(2)}) async-start(bf16[128,25,128]{2,1,0:T(8,128)(2,1)} %pad_maximum_fusion), calls=%async_computation.2 | async-start | bytes 2097152 | tf_op jit(solution)/shard_map/all_to_all | solution.py:151
  357.0 10.4 %copy-start.11 = (bf16[1024,112]{0,1:T(8,128)(2,1)S(1)}, bf16[1024,112]{0,1:T(8,128)(2,1)}, u32[]{:S(2)}) copy-start(bf16[1024,112]{0,1:T(8,128)(2,1)} %get-tuple-element.18) | copy-start | bytes 688132
  357.0 23.9 %all-to-all-start.3 = ((bf16[128,32,128]{2,1,0:T(8,128)(2,1)}), bf16[128,32,128]{2,1,0:T(8,128)(2,1)S(1)}, u32[]{:S(2)}, u32[]{:S(2)}) async-start(bf16[128,32,128]{2,1,0:T(8,128)(2,1)} %broadcast_in_dim.68), calls=%async_computation.3 | async-start | bytes 2097152 | tf_op jit(solution)/shard_map/all_to_all | solution.py:167
  367.4 6.1 %copy-start.3 = (bf16[1024,1024]{1,0:T(8,128)(2,1)S(1)}, bf16[1024,1024]{1,0:T(8,128)(2,1)}, u32[]{:S(2)}) copy-start(bf16[1024,1024]{1,0:T(8,128)(2,1)} %divide_convert_fusion) | copy-start | bytes 6291460
Sparse Core Ops, SparseCore 0:
  11.7 83.8 all-gather.4
